TPU v7x, 128 devices: a whole 4x4x4 slice. The times are simulated.
128 devices in a mesh: row: 8 (over y, core), col: 16 (over z, x).
Axes of the slice: x: 4, y: 4, z: 4, core: 2. Of those that a mesh axis runs over, the one named last changes fastest.
Arguments:
- leaf_rhs: float32 [512, 262144], P(None, ('row', 'col')), may hold values from -6 to 6
- top_rhs: float32 [512, 2048], P('col', 'row'), may hold values from -6 to 6
- leaf_inverse: float32 [1024, 256, 256], P(('row', 'col')), as said below
- leaf_blocks: float32 [1024, 4, 256, 256], P(('row', 'col')), may hold values from -0.015625 to 0.015625
- leaf_targets: int32 [1024, 4], P(('row', 'col')), may hold values from 0 to 7, as said below
- leaf_live: int32 [1024], P(('row', 'col')), may hold values from 1 to 4
- top_blocks: float32 [8, 8, 256, 256], P('row'), as said below
Outputs:
- leaf_solution: float32 [512, 262144], P(None, ('row', 'col'))
- top_solution: float32 [512, 2048], P('col', 'row')
Inputs may be any that keep to these rules, and one draw needn't show every extreme that they name: `leaf_targets`: the 4 targets of one leaf are distinct. `leaf_inverse`: lower triangular blocks with positive diagonal. `top_blocks`: diagonal entries [t, t] are lower triangular with positive diagonal.
All inputs are finite; a program needn't handle non-finite values.
Results may differ from a plain program's by a relative error of at most 0.0003.
Values sent between devices are 32-bit elements; how exact they have to be, the bound alone decides.
A program may use at most 128 MiB of HBM per device.

v0:
```python
import jax
import jax.numpy as jnp
from jax import lax
from jax.experimental import pallas as pl
from jax.experimental.pallas import tpu as pltpu
from jax.sharding import PartitionSpec as P

MESH = pl.DeviceIdType.MESH
f32 = jnp.float32
bf16 = jnp.bfloat16

PAIRS = 4
HALF = 16
LEAVES = 8
SLOTS = 4
EMPTY = LEAVES * SLOTS


def split(value):
    high = value.astype(bf16)
    return high, (value - high.astype(f32)).astype(bf16)


def products(pieces, transposed):
    left, right = [], []
    for a_high, a_low, b_high, b_low in pieces:
        left += [a_high, a_high, a_low]
        right += [b_high, b_low, b_high]
    axis = 1 if transposed else 0
    return lax.dot_general(
        jnp.concatenate(left, axis=1), jnp.concatenate(right, axis=axis),
        (((1,), (axis,)), ((), ())), preferred_element_type=f32,
    )


def whole_kernel(
    targets, live, leaf_rhs, leaf_inverse, leaf_blocks, rhs_ref, top_ref, z_ref, own_ref,
    inverse, slots, slot_high, slot_low, y_high, y_low, u_ref, x_ref, x_high, x_low, top, top_high, top_low,
    pair_in, chip_sum, first_in, middle, second_in, plane_sum, y_in, update_out, update_in, rhs, solved,
    leaf_sem, inverse_sem, slots_sem, local_sem, blocks_s, blocks_r, rhs_s, rhs_r, pair_s, pair_r,
    first_s, first_r, second_s, second_r, y_s, y_r, update_s, update_r,
    spread_s, spread_r, chunk_s, chunk_r, line_s, line_r, swap_s, swap_r,
):
    row = lax.axis_index("row")
    col = lax.axis_index("col")
    core = lax.rem(row, 2)
    y = lax.div(row, 2)
    other = 1 - core
    z = lax.div(col, 4)
    x = lax.rem(col, 4)
    mate = {"row": 2 * y + other}

    def on_y(chip):
        return {"row": 2 * chip + core}

    def on_x(step):
        return {"col": 4 * z + lax.rem(x + step, 4)}

    def on_z(step):
        return {"col": 4 * lax.rem(z + step, 4) + x}

    def remote(src, dst, send, recv, device):
        return pltpu.make_async_remote_copy(
            src_ref=src, dst_ref=dst, send_sem=send, recv_sem=recv, device_id=device, device_id_type=MESH
        )

    barrier = pltpu.get_barrier_semaphore()
    pl.semaphore_signal(barrier, inc=1, device_id=mate, device_id_type=MESH)
    for step in range(1, PAIRS):
        pl.semaphore_signal(barrier, inc=1, device_id=on_y(lax.rem(y + step, PAIRS)), device_id_type=MESH)
    for step in range(1, 4):
        pl.semaphore_signal(barrier, inc=1, device_id=on_x(step), device_id_type=MESH)
        pl.semaphore_signal(barrier, inc=1, device_id=on_z(step), device_id_type=MESH)

    def leaf_copies(k):
        column = pl.ds(pl.multiple_of(k * 256, 256), 256)
        group = pl.ds(SLOTS * k, SLOTS)
        return (
            pltpu.make_async_copy(leaf_rhs.at[:, column], z_ref.at[k], leaf_sem.at[k]),
            pltpu.make_async_copy(leaf_inverse.at[k], inverse.at[k], inverse_sem.at[k]),
            pltpu.make_async_copy(leaf_blocks.at[group], slots.at[group], slots_sem.at[k]),
        )

    for k in range(LEAVES):
        for copy in leaf_copies(k):
            copy.start()
    local_copy = pltpu.make_async_copy(top_ref, top.at[core], local_sem)
    local_copy.start()
    rhs[core] = rhs_ref[core]
    zero_block = jnp.zeros((256, 256), bf16)
    slot_high[EMPTY] = zero_block
    slot_low[EMPTY] = zero_block

    pl.semaphore_wait(barrier, 10)
    blocks_copy = remote(top_ref, top.at[core], blocks_s, blocks_r, mate)
    blocks_copy.start()
    rhs_copy = remote(rhs_ref.at[other], rhs.at[core], rhs_s, rhs_r, mate)
    rhs_copy.start()

    @pl.loop(0, LEAVES)
    def _(k):
        for copy in leaf_copies(k):
            copy.wait()
        b_high, b_low = split(inverse[k])
        for part in range(2):
            rows = pl.ds(256 * part, 256)
            a_high, a_low = split(z_ref[k, rows])
            result = products([(a_high, a_low, b_high, b_low)], True)
            z_ref[k, rows] = result
            high, low = split(result)
            y_high[k, rows] = high
            y_low[k, rows] = low
        for j in range(SLOTS):
            high, low = split(slots[SLOTS * k + j])
            slot_high[SLOTS * k + j] = high
            slot_low[SLOTS * k + j] = low

    def place_of(k, level):
        place = jnp.int32(EMPTY)
        for j in range(SLOTS):
            used = jnp.logical_and(targets[k, j] == level, live[k] > j)
            place = jnp.where(used, SLOTS * k + j, place)
        return place

    def pair_copy(p):
        return remote(u_ref.at[p, :, :, :, other], pair_in.at[p], pair_s.at[p], pair_r.at[p], mate)

    def first_copy(p, level, step):
        if level == 0:
            src, device = chip_sum.at[p, 0, :, lax.rem(x + step, 4)], on_x(step)
        else:
            src, device = chip_sum.at[p, 1, lax.rem(z + step, 4)], on_z(step)
        return remote(
            src, first_in.at[p, level, step - 1], first_s.at[p, level, step - 1], first_r.at[p, level, step - 1], device
        )

    def second_copy(p, level, step):
        if level == 0:
            src, device = middle.at[p, 0, lax.rem(z + step, 4)], on_z(step)
        else:
            src, device = middle.at[p, 1, lax.rem(x + step, 4)], on_x(step)
        return remote(
            src, second_in.at[p, level, step - 1],
            second_s.at[p, level, step - 1], second_r.at[p, level, step - 1], device,
        )

    def y_copy(p, source):
        return remote(plane_sum.at[p], y_in.at[source], y_s.at[p], y_r.at[source], on_y(p))

    both = [(level, step) for step in (2, 1, 3) for level in range(2)]

    def update_copy(source, target):
        return remote(update_out.at[target], update_in.at[source], update_s.at[target], update_r.at[source], on_y(target))

    def top_parts(column, level):
        return top_high[column, level], top_low[column, level]

    def solve_forward():
        y_in[y] = jnp.zeros((2, HALF, 256), f32)
        for chip in range(PAIRS):

            @pl.when(y != chip)
            def _():
                y_copy(chip, chip).wait_recv()

        solved[...] = rhs[...] - plane_sum[y] - (y_in[0] + y_in[1] + y_in[2] + y_in[3])
        for chip in range(PAIRS - 1):

            @pl.when(y > chip)
            def _():
                update_copy(chip, y).wait_recv()
                solved[...] = solved[...] - update_in[chip]

        first = products([split(solved[0]) + top_parts(0, 2 * y)], True)
        first_parts = split(first)
        second = solved[1] - products([first_parts + top_parts(0, 2 * y + 1)], True)
        second = products([split(second) + top_parts(1, 2 * y + 1)], True)
        second_parts = split(second)
        solved[0] = first
        solved[1] = second
        for chip in range(1, PAIRS):

            @pl.when(y < chip)
            def _():
                for level in range(2):
                    update_out[chip, level] = products(
                        [
                            first_parts + top_parts(0, 2 * chip + level),
                            second_parts + top_parts(1, 2 * chip + level),
                        ],
                        True,
                    )
                update_copy(y, chip).start()

    @pl.loop(0, 33)
    def _(quarter):
        phase = lax.rem(quarter, 4)
        round_of = lax.div(quarter, 4)

        @pl.when(quarter < 16)
        def _():
            level = lax.rem(lax.div(quarter, 2), 2)
            part = lax.rem(quarter, 2)
            rows = pl.ds(pl.multiple_of(256 * part, 256), 256)
            pieces = []
            for k in range(LEAVES):
                place = place_of(k, 2 * round_of + level)
                pieces.append((y_high[k, rows], y_low[k, rows], slot_high[place], slot_low[place]))
            u_ref[round_of, level, pl.ds(2 * part, 2)] = products(pieces, True).reshape(2, 4, 2, HALF, 256)

            @pl.when(phase == 3)
            def _():
                pair_copy(round_of).start()

        @pl.when(jnp.logical_and(phase == 1, jnp.logical_and(quarter >= 5, quarter <= 17)))
        def _():
            p = round_of - 1
            pair_copy(p).wait_recv()
            chip_sum[p] = u_ref[p, :, :, :, core] + pair_in[p]
            for level, step in both:
                first_copy(p, level, step).start()

        @pl.when(quarter == 18)
        def _():
            rhs_copy.wait_recv()
            remote(top_ref, top.at[other], blocks_s, blocks_r, mate).wait_recv()
            local_copy.wait()
            for column in range(2):

                @pl.loop(0, 8)
                def _(level):
                    high, low = split(top[column, level])
                    top_high[column, level] = high
                    top_low[column, level] = low

        @pl.when(jnp.logical_and(phase == 0, jnp.logical_and(quarter >= 16, quarter <= 28)))
        def _():
            p = round_of - 4
            for level, step in both:
                second_copy(p, level, step).wait_recv()
            plane_sum[p, 0] = middle[p, 0, z] + second_in[p, 0, 0] + second_in[p, 0, 1] + second_in[p, 0, 2]
            plane_sum[p, 1] = middle[p, 1, x] + second_in[p, 1, 0] + second_in[p, 1, 1] + second_in[p, 1, 2]

            @pl.when(y != p)
            def _():
                y_copy(p, y).start()

        @pl.when(jnp.logical_and(phase == 0, jnp.logical_and(quarter >= 12, quarter <= 24)))
        def _():
            p = round_of - 3
            for level, step in both:
                first_copy(p, level, step).wait_recv()
            middle[p, 0] = chip_sum[p, 0, :, x] + first_in[p, 0, 0] + first_in[p, 0, 1] + first_in[p, 0, 2]
            middle[p, 1] = chip_sum[p, 1, z] + first_in[p, 1, 0] + first_in[p, 1, 1] + first_in[p, 1, 2]
            for level, step in both:
                second_copy(p, level, step).start()

        @pl.when(jnp.logical_and(phase == 0, y == round_of - 5))
        def _():
            solve_forward()

    def spread(p, step):
        chunk = x_ref.at[p, :, z, x, core]
        return remote(chunk, chunk, spread_s.at[step - 1], spread_r.at[p], on_y(lax.rem(y + step, PAIRS)))

    def solve_backward():
        second = products([split(solved[1]) + top_parts(1, 2 * y + 1)], False)
        first = solved[0] - products([split(second) + top_parts(0, 2 * y + 1)], False)
        first = products([split(first) + top_parts(0, 2 * y)], False)
        x_ref[y, 0, z, x, core] = first
        x_ref[y, 1, z, x, core] = second
        for step in range(1, PAIRS):
            spread(y, step).start()

    def chunk_copy(p, level, step):
        chunk = x_ref.at[p, level, z, x, core]
        device = on_z(step) if level == 0 else on_x(step)
        return remote(chunk, chunk, chunk_s.at[p, level, step - 1], chunk_r.at[p, level, step - 1], device)

    def line_copy(p, level, step):
        if level == 0:
            line, device = x_ref.at[p, 0, :, x, core], on_x(step)
        else:
            line, device = x_ref.at[p, 1, z, :, core], on_z(step)
        return remote(line, line, line_s.at[p, level, step - 1], line_r.at[p, level, step - 1], device)

    def send_lines(p):
        for level, step in both:
            chunk_copy(p, level, step).wait_recv()
        for level, step in both:
            line_copy(p, level, step).start()

    def swap_copy(p, half):
        part = x_ref.at[p, :, :, :, half]
        return remote(part, part, swap_s.at[p], swap_r.at[p], mate)

    def send_swap(p):
        for level, step in both:
            line_copy(p, level, step).wait_recv()
        swap_copy(p, core).start()

    def arrive(p):
        @pl.when(y != p)
        def _():
            spread(p, 1).wait_recv()

        @pl.when(y < p)
        def _():
            parts = [split(x_ref[p, level, z, x, core]) for level in range(2)]
            for column in range(2):
                solved[column] = solved[column] - products(
                    [parts[level] + top_parts(column, 2 * p + level) for level in range(2)], False
                )

        if p > 0:

            @pl.when(y == p - 1)
            def _():
                solve_backward()

        for level, step in both:
            chunk_copy(p, level, step).start()

    def take_swap(p):
        swap_copy(p, other).wait_recv()
        for level in range(2):
            high, low = split(x_ref[p, level].reshape(512, 256))
            x_high[level] = high
            x_low[level] = low

    def correct(p, begin, end):
        @pl.loop(begin, end)
        def _(k):
            places = [place_of(k, 2 * p + level) for level in range(2)]
            for part in range(2):
                rows = pl.ds(256 * part, 256)
                z_ref[k, rows] = z_ref[k, rows] - products(
                    [
                        (x_high[level, rows], x_low[level, rows], slot_high[places[level]], slot_low[places[level]])
                        for level in range(2)
                    ],
                    False,
                )

    @pl.when(y == PAIRS - 1)
    def _():
        solve_backward()

    arrive(3)
    send_lines(3)
    arrive(2)
    send_lines(2)
    send_swap(3)
    arrive(1)
    take_swap(3)
    correct(3, 0, 4)
    send_lines(1)
    correct(3, 4, 8)
    send_swap(2)
    arrive(0)
    take_swap(2)
    correct(2, 0, 4)
    send_lines(0)
    correct(2, 4, 8)
    send_swap(1)
    take_swap(1)
    correct(1, 0, 8)
    send_swap(0)
    take_swap(0)
    correct(0, 0, 8)
    own_ref[...] = x_ref[y, core, z, x]

    rhs_copy.wait_send()
    blocks_copy.wait_send()
    for p in range(PAIRS):
        pair_copy(p).wait_send()
        for level, step in both:
            first_copy(p, level, step).wait_send()
            second_copy(p, level, step).wait_send()
            chunk_copy(p, level, step).wait_send()
            line_copy(p, level, step).wait_send()
        swap_copy(p, core).wait_send()

        @pl.when(y != p)
        def _():
            y_copy(p, y).wait_send()

    for chip in range(1, PAIRS):

        @pl.when(y < chip)
        def _():
            update_copy(y, chip).wait_send()

    for step in range(1, PAIRS):
        spread(y, step).wait_send()


def whole_solve(targets, live, leaf_rhs, leaf_inverse, leaf_blocks, rhs, top_blocks):
    dma = pltpu.SemaphoreType.DMA
    vmem = pl.BlockSpec(memory_space=pltpu.VMEM)
    smem = pl.BlockSpec(memory_space=pltpu.SMEM)
    hbm = pl.BlockSpec(memory_space=pl.ANY)
    return pl.pallas_call(
        whole_kernel,
        out_shape=(
            jax.ShapeDtypeStruct((LEAVES, 512, 256), f32),
            jax.ShapeDtypeStruct((2, HALF, 256), f32),
        ),
        in_specs=[smem, smem, hbm, hbm, hbm, vmem, hbm],
        out_specs=(vmem, vmem),
        scratch_shapes=[
            pltpu.VMEM((LEAVES, 256, 256), f32),
            pltpu.VMEM((LEAVES * SLOTS, 256, 256), f32),
            pltpu.VMEM((LEAVES * SLOTS + 1, 256, 256), bf16),
            pltpu.VMEM((LEAVES * SLOTS + 1, 256, 256), bf16),
            pltpu.VMEM((LEAVES, 512, 256), bf16),
            pltpu.VMEM((LEAVES, 512, 256), bf16),
            pltpu.VMEM((PAIRS, 2, 4, 4, 2, HALF, 256), f32),
            pltpu.VMEM((PAIRS, 2, 4, 4, 2, HALF, 256), f32),
            pltpu.VMEM((2, 512, 256), bf16),
            pltpu.VMEM((2, 512, 256), bf16),
            pltpu.VMEM((2, 8, 256, 256), f32),
            pltpu.VMEM((2, 8, 256, 256), bf16),
            pltpu.VMEM((2, 8, 256, 256), bf16),
            pltpu.VMEM((PAIRS, 2, 4, 4, HALF, 256), f32),
            pltpu.VMEM((PAIRS, 2, 4, 4, HALF, 256), f32),
            pltpu.VMEM((PAIRS, 2, 3, 4, HALF, 256), f32),
            pltpu.VMEM((PAIRS, 2, 4, HALF, 256), f32),
            pltpu.VMEM((PAIRS, 2, 3, HALF, 256), f32),
            pltpu.VMEM((PAIRS, 2, HALF, 256), f32),
            pltpu.VMEM((PAIRS, 2, HALF, 256), f32),
            pltpu.VMEM((PAIRS, 2, HALF, 256), f32),
            pltpu.VMEM((PAIRS, 2, HALF, 256), f32),
            pltpu.VMEM((2, HALF, 256), f32),
            pltpu.VMEM((2, HALF, 256), f32),
            dma((LEAVES,)), dma((LEAVES,)), dma((LEAVES,)),
            dma,
            dma, dma, dma, dma,
            dma((PAIRS,)), dma((PAIRS,)),
            dma((PAIRS, 2, 3)), dma((PAIRS, 2, 3)),
            dma((PAIRS, 2, 3)), dma((PAIRS, 2, 3)),
            dma((PAIRS,)), dma((PAIRS,)),
            dma((PAIRS,)), dma((PAIRS,)),
            dma((PAIRS,)), dma((PAIRS,)),
            dma((PAIRS, 2, 3)), dma((PAIRS, 2, 3)),
            dma((PAIRS, 2, 3)), dma((PAIRS, 2, 3)),
            dma((PAIRS,)), dma((PAIRS,)),
        ],
        compiler_params=pltpu.CompilerParams(
            collective_id=0, has_side_effects=True, vmem_limit_bytes=60 * 1024 * 1024
        ),
        cost_estimate=pl.CostEstimate(flops=3 * 10**10, bytes_accessed=2 * 10**7, transcendentals=0),
    )(targets, live, leaf_rhs, leaf_inverse, leaf_blocks, rhs, top_blocks)


def last_kernel(z_ref, inverse_ref, out_ref):
    parts = split(inverse_ref[0])
    for part in range(2):
        rows = pl.ds(256 * part, 256)
        out_ref[rows] = products([split(z_ref[0, rows]) + parts], False)


def last_product(z, inverse):
    return pl.pallas_call(
        last_kernel,
        out_shape=jax.ShapeDtypeStruct((512, LEAVES * 256), f32),
        grid=(LEAVES,),
        in_specs=[
            pl.BlockSpec((1, 512, 256), lambda k: (k, 0, 0)),
            pl.BlockSpec((1, 256, 256), lambda k: (k, 0, 0)),
        ],
        out_specs=pl.BlockSpec((512, 256), lambda k: (0, k)),
        cost_estimate=pl.CostEstimate(flops=16 * 10**8, bytes_accessed=10**7, transcendentals=0),
    )(z, inverse)


def on_device(leaf_rhs, top_rhs, leaf_inverse, leaf_blocks, leaf_targets, leaf_live, top_blocks):
    z, own = whole_solve(
        leaf_targets, leaf_live, leaf_rhs, leaf_inverse, leaf_blocks.reshape(LEAVES * SLOTS, 256, 256),
        top_rhs.reshape(2, HALF, 256), top_blocks[0],
    )
    return (last_product(z, leaf_inverse), own.reshape(2 * HALF, 256))


def solution(mesh):
    in_specs = (
        P(None, ("row", "col")),
        P("col", "row"),
        P(("row", "col"), None, None),
        P(("row", "col"), None, None, None),
        P(("row", "col"), None),
        P(("row", "col")),
        P("row", None, None, None),
    )
    out_specs = (P(None, ("row", "col")), P("col", "row"))
    return jax.shard_map(
        on_device, mesh=mesh, in_specs=in_specs, out_specs=out_specs, check_vma=False
    )
```

profile of v0, /device:TPU:1, one launch (start us, length us, event | category | flops | bytes accessed | tf_op | source)
XLA Modules:
  0.0 106.1 jit_solution(5651343411249236802)
XLA Ops:
  0.6 1.3 %copy.9.targets = s32[8,4]{1,0:T(8,128)} copy(s32[8,4]{0,1:T(4,128)} %param.11) | data formatting | bytes 256 | tf_op args[4]
  2.0 95.4 %shard_map.86 = (f32[8,512,256]{2,1,0:T(8,128)}, f32[2,16,256]{2,1,0:T(8,128)}) custom-call(s32[8,4]{1,0:T(8,128)} %copy.9.targets, s32[8]{0:T(128)} %live.1, f32[512,2048]{1,0:T(8,128)} %leaf_rhs.1, f32[8,256,256]{2,1,0:T(8,128)} %inverse_ref.1, f32[32,256,256]{2,1,0:T(8,128)} %bitcast.5, f32[2,16,256]{2,1,0:T(8,128)} %bitcast.7, f32[8,256,256]{2,1,0:T(8,128)} %bitcast.6), custom_call_target="tpu_custom_call" | custom-call | flops 30000001024 | bytes 20000000 | tf_op jit(solution)/shard_map/pallas_call | solution.py:403
  97.4 0.0 copy-start
  97.4 8.1 %shard_map.87 = f32[512,2048]{1,0:T(8,128)} custom-call(f32[8,512,256]{2,1,0:T(8,128)} %get-tuple-element.4.z_ref, f32[8,256,256]{2,1,0:T(8,128)} %inverse_ref.1), custom_call_target="tpu_custom_call" | custom-call | flops 1600000000 | bytes 10000000 | tf_op jit(solution)/shard_map/pallas_call | solution.py:464
  105.5 0.0 copy-done
  105.5 0.6 copy.11
Async XLA Ops:
  97.4 8.1 %copy-start = (f32[2,16,256]{2,1,0:T(8,128)S(1)}, f32[2,16,256]{2,1,0:T(8,128)}, u32[]{:S(2)}) copy-start(f32[2,16,256]{2,1,0:T(8,128)} %get-tuple-element.5) | copy-start | bytes 98308
where the time goes:
time: 107 us; the launch traced here: 106 us
  Pallas kernels  104 us (97%)
  local copies, waits for them, and re-layouts  1.97 us (2%)
    pallas_call x1, Pallas kernels, whole_solve(): pl.pallas_call(whole_kernel, out_shape=(jax.ShapeDtypeStruct((LEAVES, 512...  95.4 us
    pallas_call x1, Pallas kernels, last_product(): pl.pallas_call(last_kernel, out_shape=jax.ShapeDtypeStruct((512, LEAVES *...  8.08 us

commit v1 on v0

--- a/solution.py
+++ b/solution.py
@@ -13,6 +13,7 @@
 HALF = 16
 LEAVES = 8
 SLOTS = 4
+GROUP = 8
 EMPTY = LEAVES * SLOTS
 
 
@@ -34,10 +35,10 @@
 
 
 def whole_kernel(
-    targets, live, leaf_rhs, leaf_inverse, leaf_blocks, rhs_ref, top_ref, z_ref, own_ref,
-    inverse, slots, slot_high, slot_low, y_high, y_low, u_ref, x_ref, x_high, x_low, top, top_high, top_low,
+    targets_ref, live_ref, leaf_rhs, leaf_inverse, leaf_blocks, rhs_ref, top_ref, z_out, own_out,
+    targets, live, z_ref, inverse, slots, slot_high, slot_low, y_high, y_low, u_ref, x_ref, x_high, x_low, top, top_high, top_low,
     pair_in, chip_sum, first_in, middle, second_in, plane_sum, y_in, update_out, update_in, rhs, solved,
-    leaf_sem, inverse_sem, slots_sem, local_sem, blocks_s, blocks_r, rhs_s, rhs_r, pair_s, pair_r,
+    leaf_sem, inverse_sem, slots_sem, out_sem, local_sem, index_sem, own_sem, blocks_s, blocks_r, rhs_s, rhs_r, pair_s, pair_r,
     first_s, first_r, second_s, second_r, y_s, y_r, update_s, update_r,
     spread_s, spread_r, chunk_s, chunk_r, line_s, line_r, swap_s, swap_r,
 ):
@@ -76,26 +77,30 @@
         column = pl.ds(pl.multiple_of(k * 256, 256), 256)
         group = pl.ds(SLOTS * k, SLOTS)
         return (
-            pltpu.make_async_copy(leaf_rhs.at[:, column], z_ref.at[k], leaf_sem.at[k]),
+            pltpu.make_async_copy(leaf_rhs.at[:, :, :, column], z_ref.at[k], leaf_sem.at[k]),
             pltpu.make_async_copy(leaf_inverse.at[k], inverse.at[k], inverse_sem.at[k]),
             pltpu.make_async_copy(leaf_blocks.at[group], slots.at[group], slots_sem.at[k]),
         )
 
+    index_copies = (
+        pltpu.make_async_copy(targets_ref, targets, index_sem.at[0]),
+        pltpu.make_async_copy(live_ref, live, index_sem.at[1]),
+    )
+    for copy in index_copies:
+        copy.start()
     for k in range(LEAVES):
         for copy in leaf_copies(k):
             copy.start()
-    local_copy = pltpu.make_async_copy(top_ref, top.at[core], local_sem)
-    local_copy.start()
-    rhs[core] = rhs_ref[core]
+    local_copies = (
+        pltpu.make_async_copy(top_ref, top.at[core], local_sem.at[0]),
+        pltpu.make_async_copy(rhs_ref.at[core], rhs.at[core], local_sem.at[1]),
+    )
+    for copy in local_copies:
+        copy.start()
+    own_copy = pltpu.make_async_copy(x_ref.at[y, core, z, x], own_out, own_sem)
     zero_block = jnp.zeros((256, 256), bf16)
     slot_high[EMPTY] = zero_block
     slot_low[EMPTY] = zero_block
-
-    pl.semaphore_wait(barrier, 10)
-    blocks_copy = remote(top_ref, top.at[core], blocks_s, blocks_r, mate)
-    blocks_copy.start()
-    rhs_copy = remote(rhs_ref.at[other], rhs.at[core], rhs_s, rhs_r, mate)
-    rhs_copy.start()
 
     @pl.loop(0, LEAVES)
     def _(k):
@@ -104,9 +109,10 @@
         b_high, b_low = split(inverse[k])
         for part in range(2):
             rows = pl.ds(256 * part, 256)
-            a_high, a_low = split(z_ref[k, rows])
+            groups = pl.ds(8 * part, 8)
+            a_high, a_low = split(z_ref[k, groups].reshape(256, 256))
             result = products([(a_high, a_low, b_high, b_low)], True)
-            z_ref[k, rows] = result
+            z_ref[k, groups] = result.reshape(8, 2, HALF, 256)
             high, low = split(result)
             y_high[k, rows] = high
             y_low[k, rows] = low
@@ -115,10 +121,18 @@
             slot_high[SLOTS * k + j] = high
             slot_low[SLOTS * k + j] = low
 
+    for copy in index_copies:
+        copy.wait()
+    pl.semaphore_wait(barrier, 10)
+    blocks_copy = remote(top_ref, top.at[core], blocks_s, blocks_r, mate)
+    blocks_copy.start()
+    rhs_copy = remote(rhs_ref.at[other], rhs.at[core], rhs_s, rhs_r, mate)
+    rhs_copy.start()
+
     def place_of(k, level):
         place = jnp.int32(EMPTY)
         for j in range(SLOTS):
-            used = jnp.logical_and(targets[k, j] == level, live[k] > j)
+            used = jnp.logical_and(targets[j, k] == level, live[k] > j)
             place = jnp.where(used, SLOTS * k + j, place)
         return place
 
@@ -178,21 +192,31 @@
         second_parts = split(second)
         solved[0] = first
         solved[1] = second
-        for chip in range(1, PAIRS):
-
-            @pl.when(y < chip)
-            def _():
-                for level in range(2):
-                    update_out[chip, level] = products(
-                        [
-                            first_parts + top_parts(0, 2 * chip + level),
-                            second_parts + top_parts(1, 2 * chip + level),
-                        ],
-                        True,
-                    )
+
+        def update(chip):
+            for level in range(2):
+                update_out[chip, level] = products(
+                    [
+                        first_parts + top_parts(0, 2 * chip + level),
+                        second_parts + top_parts(1, 2 * chip + level),
+                    ],
+                    True,
+                )
+
+        update(lax.rem(y + 1, PAIRS))
+
+        @pl.when(y < PAIRS - 1)
+        def _():
+            update_copy(y, lax.rem(y + 1, PAIRS)).start()
+
+        for chip in range(2, PAIRS):
+
+            @pl.when(y < chip - 1)
+            def _():
+                update(chip)
                 update_copy(y, chip).start()
 
-    @pl.loop(0, 33)
+    @pl.loop(0, 32)
     def _(quarter):
         phase = lax.rem(quarter, 4)
         round_of = lax.div(quarter, 4)
@@ -212,7 +236,7 @@
             def _():
                 pair_copy(round_of).start()
 
-        @pl.when(jnp.logical_and(phase == 1, jnp.logical_and(quarter >= 5, quarter <= 17)))
+        @pl.when(jnp.logical_and(phase == 0, jnp.logical_and(quarter >= 4, quarter <= 16)))
         def _():
             p = round_of - 1
             pair_copy(p).wait_recv()
@@ -224,7 +248,8 @@
         def _():
             rhs_copy.wait_recv()
             remote(top_ref, top.at[other], blocks_s, blocks_r, mate).wait_recv()
-            local_copy.wait()
+            for copy in local_copies:
+                copy.wait()
             for column in range(2):
 
                 @pl.loop(0, 8)
@@ -233,9 +258,9 @@
                     top_high[column, level] = high
                     top_low[column, level] = low
 
-        @pl.when(jnp.logical_and(phase == 0, jnp.logical_and(quarter >= 16, quarter <= 28)))
-        def _():
-            p = round_of - 4
+        @pl.when(jnp.logical_and(phase == 3, jnp.logical_and(quarter >= 15, quarter <= 27)))
+        def _():
+            p = round_of - 3
             for level, step in both:
                 second_copy(p, level, step).wait_recv()
             plane_sum[p, 0] = middle[p, 0, z] + second_in[p, 0, 0] + second_in[p, 0, 1] + second_in[p, 0, 2]
@@ -245,9 +270,9 @@
             def _():
                 y_copy(p, y).start()
 
-        @pl.when(jnp.logical_and(phase == 0, jnp.logical_and(quarter >= 12, quarter <= 24)))
-        def _():
-            p = round_of - 3
+        @pl.when(jnp.logical_and(phase == 3, jnp.logical_and(quarter >= 11, quarter <= 23)))
+        def _():
+            p = round_of - 2
             for level, step in both:
                 first_copy(p, level, step).wait_recv()
             middle[p, 0] = chip_sum[p, 0, :, x] + first_in[p, 0, 0] + first_in[p, 0, 1] + first_in[p, 0, 2]
@@ -255,7 +280,7 @@
             for level, step in both:
                 second_copy(p, level, step).start()
 
-        @pl.when(jnp.logical_and(phase == 0, y == round_of - 5))
+        @pl.when(jnp.logical_and(phase == 3, y == round_of - 4))
         def _():
             solve_forward()
 
@@ -263,9 +288,9 @@
         chunk = x_ref.at[p, :, z, x, core]
         return remote(chunk, chunk, spread_s.at[step - 1], spread_r.at[p], on_y(lax.rem(y + step, PAIRS)))
 
-    def solve_backward():
-        second = products([split(solved[1]) + top_parts(1, 2 * y + 1)], False)
-        first = solved[0] - products([split(second) + top_parts(0, 2 * y + 1)], False)
+    def solve_backward(first, second):
+        second = products([split(second) + top_parts(1, 2 * y + 1)], False)
+        first = first - products([split(second) + top_parts(0, 2 * y + 1)], False)
         first = products([split(first) + top_parts(0, 2 * y)], False)
         x_ref[y, 0, z, x, core] = first
         x_ref[y, 1, z, x, core] = second
@@ -304,47 +329,65 @@
         def _():
             spread(p, 1).wait_recv()
 
-        @pl.when(y < p)
-        def _():
+        def subtract():
             parts = [split(x_ref[p, level, z, x, core]) for level in range(2)]
-            for column in range(2):
-                solved[column] = solved[column] - products(
-                    [parts[level] + top_parts(column, 2 * p + level) for level in range(2)], False
-                )
+            return [
+                solved[column]
+                - products([parts[level] + top_parts(column, 2 * p + level) for level in range(2)], False)
+                for column in range(2)
+            ]
 
         if p > 0:
 
             @pl.when(y == p - 1)
             def _():
-                solve_backward()
+                solve_backward(*subtract())
+
+        if p > 1:
+
+            @pl.when(y < p - 1)
+            def _():
+                solved[0], solved[1] = subtract()
 
         for level, step in both:
             chunk_copy(p, level, step).start()
 
-    def take_swap(p):
-        swap_copy(p, other).wait_recv()
+    def take(p, half):
         for level in range(2):
-            high, low = split(x_ref[p, level].reshape(512, 256))
+            high, low = split(x_ref[p, level, :, :, half].reshape(256, 256))
             x_high[level] = high
             x_low[level] = low
 
-    def correct(p, begin, end):
-        @pl.loop(begin, end)
-        def _(k):
-            places = [place_of(k, 2 * p + level) for level in range(2)]
-            for part in range(2):
-                rows = pl.ds(256 * part, 256)
-                z_ref[k, rows] = z_ref[k, rows] - products(
-                    [
-                        (x_high[level, rows], x_low[level, rows], slot_high[places[level]], slot_low[places[level]])
-                        for level in range(2)
-                    ],
-                    False,
-                )
+    def out_copy(k):
+        return pltpu.make_async_copy(z_ref.at[k], z_out.at[k], out_sem.at[k])
+
+    def correct(p, half, leave=False):
+        @pl.loop(0, LEAVES // GROUP)
+        def _(group):
+            for k in [GROUP * group + i for i in range(GROUP)]:
+                pieces = []
+                for level in range(2):
+                    place = place_of(k, 2 * p + level)
+                    pieces.append((x_high[level], x_low[level], slot_high[place], slot_low[place]))
+                part = z_ref[k, :, half].reshape(256, 256) - products(pieces, False)
+                z_ref[k, :, half] = part.reshape(16, HALF, 256)
+                if leave:
+                    out_copy(k).start()
+
+    def own_half(p):
+        take(p, core)
+        correct(p, core)
+
+    def other_half(p):
+        swap_copy(p, other).wait_recv()
+        if p == 0:
+            own_copy.start()
+        take(p, other)
+        correct(p, other, leave=p == 0)
 
     @pl.when(y == PAIRS - 1)
     def _():
-        solve_backward()
+        solve_backward(solved[0], solved[1])
 
     arrive(3)
     send_lines(3)
@@ -352,24 +395,24 @@
     send_lines(2)
     send_swap(3)
     arrive(1)
-    take_swap(3)
-    correct(3, 0, 4)
+    own_half(3)
     send_lines(1)
-    correct(3, 4, 8)
     send_swap(2)
     arrive(0)
-    take_swap(2)
-    correct(2, 0, 4)
+    other_half(3)
+    own_half(2)
     send_lines(0)
-    correct(2, 4, 8)
     send_swap(1)
-    take_swap(1)
-    correct(1, 0, 8)
+    other_half(2)
+    own_half(1)
+    other_half(1)
     send_swap(0)
-    take_swap(0)
-    correct(0, 0, 8)
-    own_ref[...] = x_ref[y, core, z, x]
-
+    own_half(0)
+    other_half(0)
+
+    own_copy.wait()
+    for k in range(LEAVES):
+        out_copy(k).wait()
     rhs_copy.wait_send()
     blocks_copy.wait_send()
     for p in range(PAIRS):
@@ -397,18 +440,19 @@
 
 def whole_solve(targets, live, leaf_rhs, leaf_inverse, leaf_blocks, rhs, top_blocks):
     dma = pltpu.SemaphoreType.DMA
-    vmem = pl.BlockSpec(memory_space=pltpu.VMEM)
-    smem = pl.BlockSpec(memory_space=pltpu.SMEM)
     hbm = pl.BlockSpec(memory_space=pl.ANY)
     return pl.pallas_call(
         whole_kernel,
         out_shape=(
-            jax.ShapeDtypeStruct((LEAVES, 512, 256), f32),
+            jax.ShapeDtypeStruct((LEAVES, 16, 2, HALF, 256), f32),
             jax.ShapeDtypeStruct((2, HALF, 256), f32),
         ),
-        in_specs=[smem, smem, hbm, hbm, hbm, vmem, hbm],
-        out_specs=(vmem, vmem),
+        in_specs=[hbm] * 7,
+        out_specs=(hbm, hbm),
         scratch_shapes=[
+            pltpu.SMEM((SLOTS, LEAVES), jnp.int32),
+            pltpu.SMEM((LEAVES,), jnp.int32),
+            pltpu.VMEM((LEAVES, 16, 2, HALF, 256), f32),
             pltpu.VMEM((LEAVES, 256, 256), f32),
             pltpu.VMEM((LEAVES * SLOTS, 256, 256), f32),
             pltpu.VMEM((LEAVES * SLOTS + 1, 256, 256), bf16),
@@ -417,8 +461,8 @@
             pltpu.VMEM((LEAVES, 512, 256), bf16),
             pltpu.VMEM((PAIRS, 2, 4, 4, 2, HALF, 256), f32),
             pltpu.VMEM((PAIRS, 2, 4, 4, 2, HALF, 256), f32),
-            pltpu.VMEM((2, 512, 256), bf16),
-            pltpu.VMEM((2, 512, 256), bf16),
+            pltpu.VMEM((2, 256, 256), bf16),
+            pltpu.VMEM((2, 256, 256), bf16),
             pltpu.VMEM((2, 8, 256, 256), f32),
             pltpu.VMEM((2, 8, 256, 256), bf16),
             pltpu.VMEM((2, 8, 256, 256), bf16),
@@ -433,8 +477,8 @@
             pltpu.VMEM((PAIRS, 2, HALF, 256), f32),
             pltpu.VMEM((2, HALF, 256), f32),
             pltpu.VMEM((2, HALF, 256), f32),
-            dma((LEAVES,)), dma((LEAVES,)), dma((LEAVES,)),
-            dma,
+            dma((LEAVES,)), dma((LEAVES,)), dma((LEAVES,)), dma((LEAVES,)),
+            dma((2,)), dma((2,)), dma,
             dma, dma, dma, dma,
             dma((PAIRS,)), dma((PAIRS,)),
             dma((PAIRS, 2, 3)), dma((PAIRS, 2, 3)),
@@ -453,33 +497,60 @@
     )(targets, live, leaf_rhs, leaf_inverse, leaf_blocks, rhs, top_blocks)
 
 
-def last_kernel(z_ref, inverse_ref, out_ref):
-    parts = split(inverse_ref[0])
-    for part in range(2):
-        rows = pl.ds(256 * part, 256)
-        out_ref[rows] = products([split(z_ref[0, rows]) + parts], False)
+def last_kernel(z_hbm, inverse_hbm, out_hbm, z_ref, inverse_ref, out_ref, z_sem, inverse_sem, out_sem):
+    def copies(k):
+        return (
+            pltpu.make_async_copy(z_hbm.at[k], z_ref.at[k], z_sem.at[k]),
+            pltpu.make_async_copy(inverse_hbm.at[k], inverse_ref.at[k], inverse_sem.at[k]),
+        )
+
+    def out_copy(k):
+        column = pl.ds(pl.multiple_of(k * 256, 256), 256)
+        return pltpu.make_async_copy(out_ref.at[k], out_hbm.at[:, column], out_sem.at[k])
+
+    for k in range(LEAVES):
+        for copy in copies(k):
+            copy.start()
+
+    @pl.loop(0, LEAVES)
+    def _(k):
+        for copy in copies(k):
+            copy.wait()
+        parts = split(inverse_ref[k])
+        for part in range(2):
+            rows = pl.ds(256 * part, 256)
+            out_ref[k, rows] = products([split(z_ref[k, rows]) + parts], False)
+        out_copy(k).start()
+
+    for k in range(LEAVES):
+        out_copy(k).wait()
 
 
 def last_product(z, inverse):
+    hbm = pl.BlockSpec(memory_space=pl.ANY)
+    dma = pltpu.SemaphoreType.DMA
     return pl.pallas_call(
         last_kernel,
         out_shape=jax.ShapeDtypeStruct((512, LEAVES * 256), f32),
-        grid=(LEAVES,),
-        in_specs=[
-            pl.BlockSpec((1, 512, 256), lambda k: (k, 0, 0)),
-            pl.BlockSpec((1, 256, 256), lambda k: (k, 0, 0)),
+        in_specs=[hbm, hbm],
+        out_specs=hbm,
+        scratch_shapes=[
+            pltpu.VMEM((LEAVES, 512, 256), f32),
+            pltpu.VMEM((LEAVES, 256, 256), f32),
+            pltpu.VMEM((LEAVES, 512, 256), f32),
+            dma((LEAVES,)), dma((LEAVES,)), dma((LEAVES,)),
         ],
-        out_specs=pl.BlockSpec((512, 256), lambda k: (0, k)),
+        compiler_params=pltpu.CompilerParams(vmem_limit_bytes=60 * 1024 * 1024),
         cost_estimate=pl.CostEstimate(flops=16 * 10**8, bytes_accessed=10**7, transcendentals=0),
     )(z, inverse)
 
 
 def on_device(leaf_rhs, top_rhs, leaf_inverse, leaf_blocks, leaf_targets, leaf_live, top_blocks):
     z, own = whole_solve(
-        leaf_targets, leaf_live, leaf_rhs, leaf_inverse, leaf_blocks.reshape(LEAVES * SLOTS, 256, 256),
+        leaf_targets.T, leaf_live, leaf_rhs.reshape(16, 2, HALF, LEAVES * 256), leaf_inverse, leaf_blocks.reshape(LEAVES * SLOTS, 256, 256),
         top_rhs.reshape(2, HALF, 256), top_blocks[0],
     )
-    return (last_product(z, leaf_inverse), own.reshape(2 * HALF, 256))
+    return (last_product(z.reshape(LEAVES, 512, 256), leaf_inverse), own.reshape(2 * HALF, 256))
 
 
 def solution(mesh):

time: 107 us -> 94.6 us (0.88)
  Pallas kernels: 104 us -> 93.2 us
  local copies, waits for them, and re-layouts: 1.97 us -> 0.62 us
    pallas_call x1, Pallas kernels: 95.4 us -> 88 us  [whole_solve(): pl.pallas_call(whole_kernel, out_shape=(jax.ShapeDtypeStruct((LEAVES, 16,...]
    pallas_call x1, Pallas kernels: 8.08 us -> 5.15 us  [last_product(): pl.pallas_call(last_kernel, out_shape=jax.ShapeDtypeStruct((512, LEAVES *...]
    unnamed x4 -> x3, local copies, waits for them, and re-layouts: 1.97 us -> 0.62 us
where the time goes in v1:
time: 94.6 us; the launch traced here: 94.5 us
  Pallas kernels  93.2 us (99%)
    pallas_call x1, Pallas kernels, whole_solve(): pl.pallas_call(whole_kernel, out_shape=(jax.ShapeDtypeStruct((LEAVES, 16,...  88 us
    pallas_call x1, Pallas kernels, last_product(): pl.pallas_call(last_kernel, out_shape=jax.ShapeDtypeStruct((512, LEAVES *...  5.15 us

profile of v1, /device:TPU:1, one launch (start us, length us, event | category | flops | bytes accessed | tf_op | source)
XLA Modules:
  0.0 94.5 jit_solution(15069194880469301811)
XLA Ops:
  0.6 88.0 %shard_map.86 = (f32[8,16,2,16,256]{4,3,2,1,0:T(8,128)}, f32[2,16,256]{2,1,0:T(8,128)}) custom-call(s32[4,8]{1,0:T(4,128)} %bitcast.13, s32[8]{0:T(128)} %live_ref.1, f32[16,2,16,2048]{3,2,1,0:T(8,128)} %bitcast.10, f32[8,256,256]{2,1,0:T(8,128)} %inverse_hbm.1, f32[32,256,256]{2,1,0:T(8,128)} %bitcast.9, f32[2,16,256]{2,1,0:T(8,128)} %bitcast.12, ...), custom_call_target="tpu_custom_call" | custom-call | flops 30000001024 | bytes 20000000 | tf_op jit(solution)/shard_map/pallas_call | solution.py:444
  88.7 0.0 copy-start
  88.7 5.1 %shard_map.87 = f32[512,2048]{1,0:T(8,128)} custom-call(f32[8,512,256]{2,1,0:T(8,128)} %bitcast.7, f32[8,256,256]{2,1,0:T(8,128)} %inverse_hbm.1), custom_call_target="tpu_custom_call" | custom-call | flops 1600000000 | bytes 10000000 | tf_op jit(solution)/shard_map/pallas_call | solution.py:532
  93.8 0.0 copy-done
  93.8 0.6 copy.10
Async XLA Ops:
  88.7 5.2 %copy-start = (f32[2,16,256]{2,1,0:T(8,128)S(1)}, f32[2,16,256]{2,1,0:T(8,128)}, u32[]{:S(2)}) copy-start(f32[2,16,256]{2,1,0:T(8,128)} %get-tuple-element.5) | copy-start | bytes 98308

commit v2 on v1

--- a/solution.py
+++ b/solution.py
@@ -32,6 +32,18 @@
         jnp.concatenate(left, axis=1), jnp.concatenate(right, axis=axis),
         (((1,), (axis,)), ((), ())), preferred_element_type=f32,
     )
+
+
+def small_products(pieces, transposed):
+    axis = 1 if transposed else 0
+    dims = (((1,), (axis,)), ((), ()))
+    high = jnp.concatenate([piece[0] for piece in pieces], axis=1)
+    both = jnp.concatenate([high, jnp.concatenate([piece[1] for piece in pieces], axis=1)], axis=0)
+    b_high = jnp.concatenate([piece[2] for piece in pieces], axis=axis)
+    b_low = jnp.concatenate([piece[3] for piece in pieces], axis=axis)
+    upper = lax.dot_general(both, b_high, dims, preferred_element_type=f32)
+    lower = lax.dot_general(high, b_low, dims, preferred_element_type=f32)
+    return upper[:HALF] + upper[HALF:] + lower
 
 
 def whole_kernel(
@@ -185,17 +197,17 @@
                 update_copy(chip, y).wait_recv()
                 solved[...] = solved[...] - update_in[chip]
 
-        first = products([split(solved[0]) + top_parts(0, 2 * y)], True)
+        first = small_products([split(solved[0]) + top_parts(0, 2 * y)], True)
         first_parts = split(first)
-        second = solved[1] - products([first_parts + top_parts(0, 2 * y + 1)], True)
-        second = products([split(second) + top_parts(1, 2 * y + 1)], True)
+        second = solved[1] - small_products([first_parts + top_parts(0, 2 * y + 1)], True)
+        second = small_products([split(second) + top_parts(1, 2 * y + 1)], True)
         second_parts = split(second)
         solved[0] = first
         solved[1] = second
 
         def update(chip):
             for level in range(2):
-                update_out[chip, level] = products(
+                update_out[chip, level] = small_products(
                     [
                         first_parts + top_parts(0, 2 * chip + level),
                         second_parts + top_parts(1, 2 * chip + level),
@@ -284,18 +296,21 @@
         def _():
             solve_forward()
 
-    def spread(p, step):
-        chunk = x_ref.at[p, :, z, x, core]
-        return remote(chunk, chunk, spread_s.at[step - 1], spread_r.at[p], on_y(lax.rem(y + step, PAIRS)))
+    def spread(p, level, step):
+        chunk = x_ref.at[p, level, z, x, core]
+        device = on_y(lax.rem(y + step, PAIRS))
+        return remote(chunk, chunk, spread_s.at[level, step - 1], spread_r.at[p, level], device)
+
+    def send_level(level, value):
+        x_ref[y, level, z, x, core] = value
+        for step in (3, 1, 2):
+            spread(y, level, step).start()
 
     def solve_backward(first, second):
-        second = products([split(second) + top_parts(1, 2 * y + 1)], False)
-        first = first - products([split(second) + top_parts(0, 2 * y + 1)], False)
-        first = products([split(first) + top_parts(0, 2 * y)], False)
-        x_ref[y, 0, z, x, core] = first
-        x_ref[y, 1, z, x, core] = second
-        for step in range(1, PAIRS):
-            spread(y, step).start()
+        second = small_products([split(second) + top_parts(1, 2 * y + 1)], False)
+        send_level(1, second)
+        first = first - small_products([split(second) + top_parts(0, 2 * y + 1)], False)
+        send_level(0, small_products([split(first) + top_parts(0, 2 * y)], False))
 
     def chunk_copy(p, level, step):
         chunk = x_ref.at[p, level, z, x, core]
@@ -324,33 +339,42 @@
             line_copy(p, level, step).wait_recv()
         swap_copy(p, core).start()
 
+    def subtract(p, level):
+        parts = split(x_ref[p, level, z, x, core])
+        return [
+            solved[column] - small_products([parts + top_parts(column, 2 * p + level)], False) for column in range(2)
+        ]
+
     def arrive(p):
-        @pl.when(y != p)
-        def _():
-            spread(p, 1).wait_recv()
-
-        def subtract():
-            parts = [split(x_ref[p, level, z, x, core]) for level in range(2)]
-            return [
-                solved[column]
-                - products([parts[level] + top_parts(column, 2 * p + level) for level in range(2)], False)
-                for column in range(2)
-            ]
-
+        def take_level(level):
+            @pl.when(y != p)
+            def _():
+                spread(p, level, 1).wait_recv()
+
+        take_level(1)
+        for step in (2, 1, 3):
+            chunk_copy(p, 1, step).start()
         if p > 0:
 
+            @pl.when(y < p)
+            def _():
+                solved[0], solved[1] = subtract(p, 1)
+
+        take_level(0)
+        if p > 0:
+
             @pl.when(y == p - 1)
             def _():
-                solve_backward(*subtract())
+                solve_backward(*subtract(p, 0))
 
         if p > 1:
 
             @pl.when(y < p - 1)
             def _():
-                solved[0], solved[1] = subtract()
-
-        for level, step in both:
-            chunk_copy(p, level, step).start()
+                solved[0], solved[1] = subtract(p, 0)
+
+        for step in (2, 1, 3):
+            chunk_copy(p, 0, step).start()
 
     def take(p, half):
         for level in range(2):
@@ -390,18 +414,18 @@
         solve_backward(solved[0], solved[1])
 
     arrive(3)
+    arrive(2)
     send_lines(3)
-    arrive(2)
+    arrive(1)
     send_lines(2)
     send_swap(3)
-    arrive(1)
+    arrive(0)
+    send_lines(1)
     own_half(3)
-    send_lines(1)
     send_swap(2)
-    arrive(0)
     other_half(3)
+    send_lines(0)
     own_half(2)
-    send_lines(0)
     send_swap(1)
     other_half(2)
     own_half(1)
@@ -435,7 +459,8 @@
             update_copy(y, chip).wait_send()
 
     for step in range(1, PAIRS):
-        spread(y, step).wait_send()
+        for level in range(2):
+            spread(y, level, step).wait_send()
 
 
 def whole_solve(targets, live, leaf_rhs, leaf_inverse, leaf_blocks, rhs, top_blocks):
@@ -485,7 +510,7 @@
             dma((PAIRS, 2, 3)), dma((PAIRS, 2, 3)),
             dma((PAIRS,)), dma((PAIRS,)),
             dma((PAIRS,)), dma((PAIRS,)),
-            dma((PAIRS,)), dma((PAIRS,)),
+            dma((2, 3)), dma((PAIRS, 2)),
             dma((PAIRS, 2, 3)), dma((PAIRS, 2, 3)),
             dma((PAIRS, 2, 3)), dma((PAIRS, 2, 3)),
             dma((PAIRS,)), dma((PAIRS,)),

time: 94.6 us -> 88.5 us (0.936)
  Pallas kernels: 93.2 us -> 87.1 us
    pallas_call x1, Pallas kernels: 88 us -> 82 us  [whole_solve(): pl.pallas_call(whole_kernel, out_shape=(jax.ShapeDtypeStruct((LEAVES, 16,...]
where the time goes in v2:
time: 88.5 us; the launch traced here: 88.4 us
  Pallas kernels  87.1 us (98%)
    pallas_call x1, Pallas kernels, whole_solve(): pl.pallas_call(whole_kernel, out_shape=(jax.ShapeDtypeStruct((LEAVES, 16,...  82 us
    pallas_call x1, Pallas kernels, last_product(): pl.pallas_call(last_kernel, out_shape=jax.ShapeDtypeStruct((512, LEAVES *...  5.15 us

profile of v2, /device:TPU:1, one launch (start us, length us, event | category | flops | bytes accessed | tf_op | source)
XLA Modules:
  0.0 88.4 jit_solution(2241230529183120840)
XLA Ops:
  0.6 82.0 %shard_map.86 = (f32[8,16,2,16,256]{4,3,2,1,0:T(8,128)}, f32[2,16,256]{2,1,0:T(8,128)}) custom-call(s32[4,8]{1,0:T(4,128)} %bitcast.13, s32[8]{0:T(128)} %live_ref.1, f32[16,2,16,2048]{3,2,1,0:T(8,128)} %bitcast.10, f32[8,256,256]{2,1,0:T(8,128)} %inverse_hbm.1, f32[32,256,256]{2,1,0:T(8,128)} %bitcast.9, f32[2,16,256]{2,1,0:T(8,128)} %bitcast.12, ...), custom_call_target="tpu_custom_call" | custom-call | flops 30000001024 | bytes 20000000 | tf_op jit(solution)/shard_map/pallas_call | solution.py:469
  82.6 0.0 copy-start
  82.6 5.1 %shard_map.87 = f32[512,2048]{1,0:T(8,128)} custom-call(f32[8,512,256]{2,1,0:T(8,128)} %bitcast.7, f32[8,256,256]{2,1,0:T(8,128)} %inverse_hbm.1), custom_call_target="tpu_custom_call" | custom-call | flops 1600000000 | bytes 10000000 | tf_op jit(solution)/shard_map/pallas_call | solution.py:557
  87.8 0.0 copy-done
  87.8 0.6 copy.10
Async XLA Ops:
  82.6 5.2 %copy-start = (f32[2,16,256]{2,1,0:T(8,128)S(1)}, f32[2,16,256]{2,1,0:T(8,128)}, u32[]{:S(2)}) copy-start(f32[2,16,256]{2,1,0:T(8,128)} %get-tuple-element.5) | copy-start | bytes 98308

commit v3 on v2

--- a/solution.py
+++ b/solution.py
@@ -352,27 +352,27 @@
                 spread(p, level, 1).wait_recv()
 
         take_level(1)
+        if p > 0:
+
+            @pl.when(y < p)
+            def _():
+                solved[0], solved[1] = subtract(p, 1)
+
+        take_level(0)
+        if p > 0:
+
+            @pl.when(y == p - 1)
+            def _():
+                solve_backward(*subtract(p, 0))
+
+        if p > 1:
+
+            @pl.when(y < p - 1)
+            def _():
+                solved[0], solved[1] = subtract(p, 0)
+
         for step in (2, 1, 3):
             chunk_copy(p, 1, step).start()
-        if p > 0:
-
-            @pl.when(y < p)
-            def _():
-                solved[0], solved[1] = subtract(p, 1)
-
-        take_level(0)
-        if p > 0:
-
-            @pl.when(y == p - 1)
-            def _():
-                solve_backward(*subtract(p, 0))
-
-        if p > 1:
-
-            @pl.when(y < p - 1)
-            def _():
-                solved[0], solved[1] = subtract(p, 0)
-
         for step in (2, 1, 3):
             chunk_copy(p, 0, step).start()
 

time: 88.5 us -> 88.1 us (level)
  no operation moved by 1% of the time
where the time goes in v3:
time: 88.1 us; the launch traced here: 88 us
  Pallas kernels  86.7 us (98%)
    pallas_call x1, Pallas kernels, whole_solve(): pl.pallas_call(whole_kernel, out_shape=(jax.ShapeDtypeStruct((LEAVES, 16,...  81.5 us
    pallas_call x1, Pallas kernels, last_product(): pl.pallas_call(last_kernel, out_shape=jax.ShapeDtypeStruct((512, LEAVES *...  5.15 us

profile of v3, /device:TPU:1, one launch (start us, length us, event | category | flops | bytes accessed | tf_op | source)
XLA Modules:
  0.0 88.0 jit_solution(16740124981217679402)
XLA Ops:
  0.6 81.5 %shard_map.86 = (f32[8,16,2,16,256]{4,3,2,1,0:T(8,128)}, f32[2,16,256]{2,1,0:T(8,128)}) custom-call(s32[4,8]{1,0:T(4,128)} %bitcast.13, s32[8]{0:T(128)} %live_ref.1, f32[16,2,16,2048]{3,2,1,0:T(8,128)} %bitcast.10, f32[8,256,256]{2,1,0:T(8,128)} %inverse_hbm.1, f32[32,256,256]{2,1,0:T(8,128)} %bitcast.9, f32[2,16,256]{2,1,0:T(8,128)} %bitcast.12, ...), custom_call_target="tpu_custom_call" | custom-call | flops 30000001024 | bytes 20000000 | tf_op jit(solution)/shard_map/pallas_call | solution.py:469
  82.2 0.0 copy-start
  82.2 5.1 %shard_map.87 = f32[512,2048]{1,0:T(8,128)} custom-call(f32[8,512,256]{2,1,0:T(8,128)} %bitcast.7, f32[8,256,256]{2,1,0:T(8,128)} %inverse_hbm.1), custom_call_target="tpu_custom_call" | custom-call | flops 1600000000 | bytes 10000000 | tf_op jit(solution)/shard_map/pallas_call | solution.py:557
  87.4 0.0 copy-done
  87.4 0.6 copy.10
Async XLA Ops:
  82.2 5.2 %copy-start = (f32[2,16,256]{2,1,0:T(8,128)S(1)}, f32[2,16,256]{2,1,0:T(8,128)}, u32[]{:S(2)}) copy-start(f32[2,16,256]{2,1,0:T(8,128)} %get-tuple-element.5) | copy-start | bytes 98308
